TPU v7x, 32 devices: a whole 2x2x4 slice. The times are simulated.
32 devices in a mesh: dp: 8 (over y, x, core), fsdp: 4 (over z).
Axes of the slice: x: 2, y: 2, z: 4, core: 2. Of those that a mesh axis runs over, the one named last changes fastest.
Arguments:
- tokens: bfloat16 [128, 256, 384], P(('dp', 'fsdp')), may hold values from -4 to 4, as said below
- cond: bfloat16 [128, 384], P(('dp', 'fsdp')), may hold values from -4 to 4, as said below
- cotangent: bfloat16 [128, 256, 384], P(('dp', 'fsdp')), may hold values from -4 to 4, as said below
- keep_mask: int32 [128], P(('dp', 'fsdp')), may hold values 0 or 1
- w_ada: bfloat16 [2, 384, 2304], P(None, 'fsdp'), may hold values from -0.20412415 to 0.20412415, as said below
- w_qkv: bfloat16 [2, 384, 1152], P(None, 'fsdp'), may hold values from -0.20412415 to 0.20412415, as said below
- w_proj: bfloat16 [2, 384, 384], P(None, 'fsdp'), may hold values from -1.6329932 to 1.6329932, as said below
- w_up: bfloat16 [2, 384, 1536], P(None, 'fsdp'), may hold values from -0.20412415 to 0.20412415, as said below
- w_down: bfloat16 [2, 1536, 384], P(None, 'fsdp'), may hold values from -0.102062073 to 0.102062073, as said below
Outputs:
- output: bfloat16 [128, 256, 384], P(('dp', 'fsdp'))
- grad_tokens: float32 [128, 256, 384], P(('dp', 'fsdp'))
- grad_cond: float32 [128, 384], P(('dp', 'fsdp'))
- grad_ada: float32 [2, 384, 2304], P(None, 'fsdp')
- grad_qkv: float32 [2, 384, 1152], P(None, 'fsdp')
- grad_proj: float32 [2, 384, 384], P(None, 'fsdp')
- grad_up: float32 [2, 384, 1536], P(None, 'fsdp')
- grad_down: float32 [2, 1536, 384], P(None, 'fsdp')
Inputs may be any that keep to these rules, and one draw needn't show every extreme that they name: `tokens`: independent entries of mean zero and deviation one. `cond`: independent entries of mean zero and deviation one. `cotangent`: independent entries of mean zero and deviation one. `w_ada`: independent entries of mean zero and deviation 384^-0.5. `w_qkv`: independent entries of mean zero and deviation 384^-0.5. `w_proj`: independent entries of mean zero. `w_up`: independent entries of mean zero and deviation 384^-0.5. `w_down`: independent entries of mean zero and deviation 1536^-0.5.
All inputs are finite; a program needn't handle non-finite values. No bound on the sum of `keep_mask` on one device may be relied on, other than what follows from the above.
Results may differ from a plain program's by a relative error of at most 0.014.
Values may be sent and summed in bfloat16 or wider, within the bound.
A program may use at most 192 MiB of HBM per device.

v0:
```python
from functools import partial

import jax
import jax.numpy as jnp
from jax import lax
from jax.sharding import PartitionSpec as P

HEADS = 6


def modulate(values, shift, scale):
    center = jnp.mean(values, axis=-1, keepdims=True)
    centered = values - center
    spread = jnp.mean(centered * centered, axis=-1, keepdims=True)
    return centered * lax.rsqrt(spread + 1e-06) * (1.0 + scale[:, None, :]) + shift[:, None, :]


def block_forward(state, cond_act, w_ada, w_qkv, w_proj, w_up, w_down):
    images, length, width = state.shape
    head_size = width // HEADS
    modulation = jnp.dot(cond_act, w_ada, preferred_element_type=jnp.float32)
    pieces = jnp.split(modulation, 6, axis=1)
    first_in = modulate(state, pieces[0], pieces[1]).astype(jnp.bfloat16)
    qkv = jnp.einsum("ild,de->ile", first_in, w_qkv, preferred_element_type=jnp.float32).astype(
        jnp.bfloat16
    )
    qkv = qkv.reshape(images, length, 3, HEADS, head_size)
    queries = qkv[:, :, 0]
    key_rows = qkv[:, :, 1]
    values = qkv[:, :, 2]
    scores = jnp.einsum(
        "iqhe,ikhe->ihqk", queries, key_rows, preferred_element_type=jnp.float32
    ) * head_size ** (-0.5)
    probs = jax.nn.softmax(scores, axis=-1)
    probs_low = probs.astype(jnp.bfloat16)
    mixed = jnp.einsum("ihqk,ikhe->iqhe", probs_low, values, preferred_element_type=jnp.float32)
    mixed = mixed.astype(jnp.bfloat16).reshape(images, length, width)
    attended = jnp.einsum("ild,de->ile", mixed, w_proj, preferred_element_type=jnp.float32)
    middle = state + pieces[2][:, None, :] * attended
    second_in = modulate(middle, pieces[3], pieces[4]).astype(jnp.bfloat16)
    hidden_pre = jnp.einsum("ild,df->ilf", second_in, w_up, preferred_element_type=jnp.float32)
    activated = jax.nn.gelu(hidden_pre, approximate=True).astype(jnp.bfloat16)
    branch_out = jnp.einsum("ilf,fd->ild", activated, w_down, preferred_element_type=jnp.float32)
    result = middle + pieces[5][:, None, :] * branch_out
    saved = (
        pieces,
        first_in,
        queries,
        key_rows,
        values,
        probs,
        probs_low,
        mixed,
        attended,
        middle,
        second_in,
        hidden_pre,
        activated,
        branch_out,
    )
    return (result, saved)


def block_backward(state, cond_act, w_ada, w_qkv, w_proj, w_up, w_down, incoming):
    images, length, width = state.shape
    head_size = width // HEADS
    scaling = head_size ** (-0.5)
    result, saved = block_forward(state, cond_act, w_ada, w_qkv, w_proj, w_up, w_down)
    (
        pieces,
        first_in,
        queries,
        key_rows,
        values,
        probs,
        probs_low,
        mixed,
        attended,
        middle,
        second_in,
        hidden_pre,
        activated,
        branch_out,
    ) = saved
    grad_gate2 = jnp.sum(incoming * branch_out, axis=1)
    d_branch = (incoming * pieces[5][:, None, :]).astype(jnp.bfloat16)
    g_down = jnp.einsum("ilf,ild->fd", activated, d_branch, preferred_element_type=jnp.float32)
    d_activated = jnp.einsum("ild,fd->ilf", d_branch, w_down, preferred_element_type=jnp.float32)
    gelu_vals, gelu_pull = jax.vjp(partial(jax.nn.gelu, approximate=True), hidden_pre)
    d_hidden = gelu_pull(d_activated)[0].astype(jnp.bfloat16)
    g_up = jnp.einsum("ild,ilf->df", second_in, d_hidden, preferred_element_type=jnp.float32)
    d_second = jnp.einsum("ilf,df->ild", d_hidden, w_up, preferred_element_type=jnp.float32)
    norm_vals, norm_pull = jax.vjp(modulate, middle, pieces[3], pieces[4])
    middle_part, grad_shift2, grad_scale2 = norm_pull(d_second)
    d_middle = incoming + middle_part
    grad_gate1 = jnp.sum(d_middle * attended, axis=1)
    d_attended = (d_middle * pieces[2][:, None, :]).astype(jnp.bfloat16)
    g_proj = jnp.einsum("ild,ile->de", mixed, d_attended, preferred_element_type=jnp.float32)
    d_mixed = jnp.einsum("ile,de->ild", d_attended, w_proj, preferred_element_type=jnp.float32)
    d_mixed = d_mixed.astype(jnp.bfloat16).reshape(images, length, HEADS, head_size)
    d_probs = jnp.einsum("iqhe,ikhe->ihqk", d_mixed, values, preferred_element_type=jnp.float32)
    grad_values = jnp.einsum(
        "ihqk,iqhe->ikhe", probs_low, d_mixed, preferred_element_type=jnp.float32
    )
    d_scores = probs * (d_probs - jnp.sum(probs * d_probs, axis=-1, keepdims=True))
    d_scores = d_scores.astype(jnp.bfloat16)
    grad_queries = (
        jnp.einsum("ihqk,ikhe->iqhe", d_scores, key_rows, preferred_element_type=jnp.float32)
        * scaling
    )
    grad_keys = (
        jnp.einsum("ihqk,iqhe->ikhe", d_scores, queries, preferred_element_type=jnp.float32)
        * scaling
    )
    d_qkv = jnp.stack([grad_queries, grad_keys, grad_values], axis=2).astype(jnp.bfloat16)
    d_qkv = d_qkv.reshape(images, length, 3 * width)
    g_qkv = jnp.einsum("ild,ile->de", first_in, d_qkv, preferred_element_type=jnp.float32)
    d_first = jnp.einsum("ile,de->ild", d_qkv, w_qkv, preferred_element_type=jnp.float32)
    first_vals, first_pull = jax.vjp(modulate, state, pieces[0], pieces[1])
    state_part, grad_shift1, grad_scale1 = first_pull(d_first)
    outgoing = d_middle + state_part
    d_modulation = jnp.concatenate(
        [grad_shift1, grad_scale1, grad_gate1, grad_shift2, grad_scale2, grad_gate2], axis=1
    ).astype(jnp.bfloat16)
    g_ada = jnp.einsum("id,ie->de", cond_act, d_modulation, preferred_element_type=jnp.float32)
    d_cond_act = jnp.einsum("ie,de->id", d_modulation, w_ada, preferred_element_type=jnp.float32)
    return (outgoing, d_cond_act, g_ada, g_qkv, g_proj, g_up, g_down)


def body(tokens, cond, cotangent, keep_mask, w_ada, w_qkv, w_proj, w_up, w_down):
    blocks = w_ada.shape[0]
    cond_f = cond.astype(jnp.float32)
    cond_act = jax.nn.silu(cond_f).astype(jnp.bfloat16)
    current = tokens.astype(jnp.float32)
    inputs = []
    for index in range(blocks):
        inputs.append(current)
        gathered = (
            lax.all_gather(w_ada[index], "fsdp", axis=0, tiled=True),
            lax.all_gather(w_qkv[index], "fsdp", axis=0, tiled=True),
            lax.all_gather(w_proj[index], "fsdp", axis=0, tiled=True),
            lax.all_gather(w_up[index], "fsdp", axis=0, tiled=True),
            lax.all_gather(w_down[index], "fsdp", axis=0, tiled=True),
        )
        current, saved = block_forward(current, cond_act, *gathered)
    output = current.astype(jnp.bfloat16)
    incoming = cotangent.astype(jnp.float32) * keep_mask.astype(jnp.float32)[:, None, None]
    cond_grad_sum = jnp.zeros(cond_f.shape, jnp.float32)
    collected = [None] * blocks
    for index in reversed(range(blocks)):
        gathered = (
            lax.all_gather(w_ada[index], "fsdp", axis=0, tiled=True),
            lax.all_gather(w_qkv[index], "fsdp", axis=0, tiled=True),
            lax.all_gather(w_proj[index], "fsdp", axis=0, tiled=True),
            lax.all_gather(w_up[index], "fsdp", axis=0, tiled=True),
            lax.all_gather(w_down[index], "fsdp", axis=0, tiled=True),
        )
        incoming, d_cond_act, g_ada, g_qkv, g_proj, g_up, g_down = block_backward(
            inputs[index], cond_act, *gathered, incoming
        )
        cond_grad_sum = cond_grad_sum + d_cond_act
        shard_ada, shard_qkv, shard_proj, shard_up, shard_down = (
            lax.psum_scatter(
                g_ada.astype(jnp.bfloat16), "fsdp", scatter_dimension=0, tiled=True
            ).astype(jnp.float32),
            lax.psum_scatter(
                g_qkv.astype(jnp.bfloat16), "fsdp", scatter_dimension=0, tiled=True
            ).astype(jnp.float32),
            lax.psum_scatter(
                g_proj.astype(jnp.bfloat16), "fsdp", scatter_dimension=0, tiled=True
            ).astype(jnp.float32),
            lax.psum_scatter(
                g_up.astype(jnp.bfloat16), "fsdp", scatter_dimension=0, tiled=True
            ).astype(jnp.float32),
            lax.psum_scatter(
                g_down.astype(jnp.bfloat16), "fsdp", scatter_dimension=0, tiled=True
            ).astype(jnp.float32),
        )
        collected[index] = (shard_ada, shard_qkv, shard_proj, shard_up, shard_down)
    stacked = [
        jnp.stack([collected[index][member] for index in range(blocks)]) for member in range(5)
    ]
    stacked = lax.psum((stacked[0], stacked[1], stacked[2], stacked[3], stacked[4]), "dp")
    silu_vals, silu_pull = jax.vjp(jax.nn.silu, cond_f)
    grad_cond = silu_pull(cond_grad_sum)[0]
    return (output, incoming, grad_cond, stacked[0], stacked[1], stacked[2], stacked[3], stacked[4])


def solution(mesh):
    placed = (
        P(("dp", "fsdp"), None, None),
        P(("dp", "fsdp"), None),
        P(("dp", "fsdp"), None, None),
        P(("dp", "fsdp")),
        P(None, "fsdp", None),
        P(None, "fsdp", None),
        P(None, "fsdp", None),
        P(None, "fsdp", None),
        P(None, "fsdp", None),
    )
    return jax.shard_map(
        body,
        mesh=mesh,
        in_specs=placed,
        out_specs=(
            P(("dp", "fsdp"), None, None),
            P(("dp", "fsdp"), None, None),
            P(("dp", "fsdp"), None),
            P(None, "fsdp", None),
            P(None, "fsdp", None),
            P(None, "fsdp", None),
            P(None, "fsdp", None),
            P(None, "fsdp", None),
        ),
        check_vma=False,
    )
```

profile of v0, /device:TPU:0, one launch (start us, length us, event | category | flops | bytes accessed | tf_op | source)
XLA Modules:
  0.0 703.1 jit_solution(4661462757340711307)
XLA Ops:
  14.7 18.6 %all-gather.7 = bf16[1,384,384]{2,1,0:T(8,128)(2,1)} all-gather(bf16[1,96,384]{2,1,0:T(8,128)(2,1)S(1)} %get-tuple-element.49), channel_id=9, replica_groups=mesh['dp'=8,'fsdp'=4] {'fsdp'}, dimensions={1}, use_global_device_ids=true | all-gather | bytes 368640 | tf_op jit(solution)/shard_map/all_gather | solution.py:141
  33.3 17.4 %all-gather.2 = bf16[1,384,384]{2,1,0:T(8,128)(2,1)S(1)} all-gather(bf16[1,96,384]{2,1,0:T(8,128)(2,1)S(1)} %get-tuple-element.50), channel_id=4, replica_groups=mesh['dp'=8,'fsdp'=4] {'fsdp'}, dimensions={1}, use_global_device_ids=true | all-gather | bytes 368640 | tf_op jit(solution)/shard_map/all_gather | solution.py:141
  50.8 25.9 %all-gather.6 = bf16[1,384,1152]{2,1,0:T(8,128)(2,1)} all-gather(bf16[1,96,1152]{2,1,0:T(8,128)(2,1)S(1)} %get-tuple-element.47), channel_id=8, replica_groups=mesh['dp'=8,'fsdp'=4] {'fsdp'}, dimensions={1}, use_global_device_ids=true | all-gather | bytes 1105920 | tf_op jit(solution)/shard_map/all_gather | solution.py:140
  76.7 28.5 %all-gather.1 = bf16[1,384,1152]{2,1,0:T(8,128)(2,1)S(1)} all-gather(bf16[1,96,1152]{2,1,0:T(8,128)(2,1)S(1)} %get-tuple-element.48), channel_id=3, replica_groups=mesh['dp'=8,'fsdp'=4] {'fsdp'}, dimensions={1}, use_global_device_ids=true | all-gather | bytes 1105920 | tf_op jit(solution)/shard_map/all_gather | solution.py:140
  107.3 13.8 %all-gather.23.cloned.1.call-done = bf16[1,384,2304]{2,1,0:T(8,128)(2,1)} async-done(((bf16[1,96,2304]{2,1,0:T(8,128)(2,1)}), bf16[1,384,2304]{2,1,0:T(8,128)(2,1)}) %all-gather.23.cloned.1.call-update) | async-done | bytes 1769488 | tf_op jit(solution)/shard_map/all_gather | solution.py:139
  123.6 3.0 convolution_convert_fusion.3
  126.6 4.3 copy.43
  133.3 4.8 fusion.148
  138.1 2.5 fusion.57
  143.0 10.1 %all-gather.19.cloned.1.call-done = bf16[1,384,1536]{2,1,0:T(8,128)(2,1)} async-done(((bf16[1,96,1536]{2,1,0:T(8,128)(2,1)}), bf16[1,384,1536]{2,1,0:T(8,128)(2,1)}) %all-gather.19.cloned.1.call-update) | async-done | bytes 1179664 | tf_op jit(solution)/shard_map/all_gather | solution.py:142
  153.2 5.8 fusion.93
  159.0 25.8 %all-gather.21.cloned.1.call-done = bf16[1,1536,384]{2,1,0:T(8,128)(2,1)} async-done(((bf16[1,384,384]{2,1,0:T(8,128)(2,1)}), bf16[1,1536,384]{2,1,0:T(8,128)(2,1)}) %all-gather.21.cloned.1.call-update) | async-done | bytes 1179664 | tf_op jit(solution)/shard_map/all_gather | solution.py:143
  184.8 6.4 fusion.139
  192.9 3.1 convolution_convert_fusion.2
  196.1 4.3 copy.49
  202.8 5.0 fusion.149
  207.8 2.6 fusion.63
  215.8 5.7 fusion.86
  221.5 25.8 %all-gather.27.cloned.1.call-done = bf16[1,1536,384]{2,1,0:T(8,128)(2,1)} async-done(((bf16[1,384,384]{2,1,0:T(8,128)(2,1)}), bf16[1,1536,384]{2,1,0:T(8,128)(2,1)}) %all-gather.27.cloned.1.call-update) | async-done | bytes 1179664 | tf_op jit(solution)/shard_map/all_gather | solution.py:143
  247.3 7.5 %fusion.15 = bf16[4,256,1536]{2,1,0:T(8,128)(2,1)S(1)} fusion(f32[4,256,1536]{2,1,0:T(8,128)} %fusion.86, bf16[1,1536,384]{2,1,0:T(8,128)(2,1)} %all-gather.27.cloned.1.call-done, bf16[4,256,384]{2,1,0:T(8,128)(2,1)} %param.11, f32[4]{0:T(128)} %convert_element_type.173, f32[4,384]{1,0:T(4,128)} %get-tuple-element.51), kind=kOutput, calls=%fused_computation.19 | convolution fusion | flops 1240989696 | bytes 11409424 | tf_op jit(solution)/shard_map/ild,fd->ilf/dot_general | solution.py:88
  260.0 4.9 multiply_reduce_fusion.7
  267.5 3.0 convolution_convert_fusion.5
  272.8 5.1 fusion.69
  277.9 6.8 multiply_reduce_fusion.1
  284.7 4.3 multiply_convert_fusion.1
  302.1 5.3 fusion.8
  316.6 2.9 fusion.79
  319.6 7.2 %multiply_reduce_fusion = (f32[4,6,256]{2,1,0:T(8,128)S(1)}, f32[4,6,256,256]{2,3,1,0:T(8,128)}) fusion(f32[4,6,256,256]{2,3,1,0:T(8,128)} %copy-done.6, f32[4,6,256]{2,1,0:T(8,128)S(1)} %get-tuple-element.63, bf16[4,256,6,64]{1,3,2,0:T(8,128)(2,1)} %bitcast.242, bf16[4,256,3,6,64]{1,4,3,2,0:T(8,128)(2,1)} %bitcast.224), kind=kOutput, calls=%fused_computation.21 | convolution fusion | flops 206039040 | bytes 14204928 | tf_op jit(solution)/shard_map/iqhe,ikhe->ihqk/dot_general | solution.py:101
  326.8 2.5 fusion.25
  329.6 6.3 multiply_convert_fusion
  338.1 3.9 fusion.72
  344.1 2.5 fusion.24
  346.7 6.8 fusion.29
  353.6 7.1 %fusion.28 = bf16[1536,384]{1,0:T(8,128)(2,1)} fusion(f32[4,256,384]{2,1,0:T(8,128)} %copy-done.16, f32[4,384]{1,0:T(4,128)S(1)} %copy-done.77, f32[4,256,1536]{2,1,0:T(8,128)} %fusion.93), kind=kOutput, calls=%fused_computation.50 | convolution fusion | flops 1223491584 | bytes 9050112 | tf_op jit(solution)/shard_map/ilf,ild->fd/dot_general | solution.py:87
  360.8 4.5 fusion.27
  365.7 4.5 fusion.26
  372.3 3.7 fusion.48
  380.8 9.0 %reduce-scatter.15.cloned.1.call-done = bf16[96,1152]{1,0:T(8,128)(2,1)} async-done(((bf16[384,1152]{1,0:T(8,128)(2,1)}), bf16[96,1152]{1,0:T(8,128)(2,1)}) %reduce-scatter.15.cloned.1.call-update) | async-done | bytes 221200 | tf_op jit(solution)/shard_map/reduce_scatter | solution.py:166
  391.8 28.5 %reduce-scatter.29.cloned.1.call-done = bf16[384,384]{1,0:T(8,128)(2,1)} async-done(((bf16[1536,384]{1,0:T(8,128)(2,1)}), bf16[384,384]{1,0:T(8,128)(2,1)}) %reduce-scatter.29.cloned.1.call-update) | async-done | bytes 294928 | tf_op jit(solution)/shard_map/reduce_scatter | solution.py:175
  420.3 30.1 %reduce-scatter.27.cloned.1.call-done = bf16[384,384]{1,0:T(8,128)(2,1)} async-done(((bf16[1536,384]{1,0:T(8,128)(2,1)}), bf16[384,384]{1,0:T(8,128)(2,1)}) %reduce-scatter.27.cloned.1.call-update) | async-done | bytes 294928 | tf_op jit(solution)/shard_map/reduce_scatter | solution.py:175
  452.6 28.7 %reduce-scatter.25.cloned.1.call-done = bf16[96,1536]{1,0:T(8,128)(2,1)} async-done(((bf16[384,1536]{1,0:T(8,128)(2,1)}), bf16[96,1536]{1,0:T(8,128)(2,1)}) %reduce-scatter.25.cloned.1.call-update) | async-done | bytes 294928 | tf_op jit(solution)/shard_map/reduce_scatter | solution.py:172
  481.2 30.7 %reduce-scatter.23.cloned.1.call-done = bf16[96,1536]{1,0:T(8,128)(2,1)} async-done(((bf16[384,1536]{1,0:T(8,128)(2,1)}), bf16[96,1536]{1,0:T(8,128)(2,1)}) %reduce-scatter.23.cloned.1.call-update) | async-done | bytes 294928 | tf_op jit(solution)/shard_map/reduce_scatter | solution.py:172
  514.0 37.7 %reduce-scatter.13.cloned.1.call-done = bf16[96,2304]{1,0:T(8,128)(2,1)} async-done(((bf16[384,2304]{1,0:T(8,128)(2,1)}), bf16[96,2304]{1,0:T(8,128)(2,1)}) %reduce-scatter.13.cloned.1.call-update) | async-done | bytes 442384 | tf_op jit(solution)/shard_map/reduce_scatter | solution.py:163
  551.8 39.8 %reduce-scatter.11.cloned.1.call-done = bf16[96,2304]{1,0:T(8,128)(2,1)} async-done(((bf16[384,2304]{1,0:T(8,128)(2,1)}), bf16[96,2304]{1,0:T(8,128)(2,1)}) %reduce-scatter.11.cloned.1.call-update) | async-done | bytes 442384 | tf_op jit(solution)/shard_map/reduce_scatter | solution.py:163
  591.6 2.5 maximum_convert_fusion
  597.5 2.7 add_add_fusion.4
  600.2 89.1 %all-reduce.3.cloned.1.call-done = (f32[2,96,2304]{2,1,0:T(8,128)}, f32[2,96,1152]{2,1,0:T(8,128)}, f32[2,96,384]{2,1,0:T(8,128)}, f32[2,96,1536]{2,1,0:T(8,128)}, f32[2,384,384]{2,1,0:T(8,128)}) async-done(((f32[2,96,2304]{2,1,0:T(8,128)}, f32[2,96,1152]{2,1,0:T(8,128)}, f32[2,96,384]{2,1,0:T(8,128)}, f32[2,96,1536]{2,1,0:T(8,128)}, f32[2,384,384]{2,1,0:T(8,128)}), (f32[2,96,2304]{2,1,0:T(8,128)}, ...) | async-done | bytes 5308432 | tf_op jit(solution)/shard_map/psum | solution.py:183
  689.3 2.9 copy.116
  (313 shorter events, 83.7 us)
Async XLA Ops:
  7.2 98.0 %all-gather.17.cloned.1.call-start = ((), (), s32[]{:S(2)}) async-start(), calls=%async_computation.20 | async-start | bytes 2211840 | tf_op jit(solution)/shard_map/all_gather | solution.py:139
  9.4 111.7 %all-gather.23.cloned.1.call-start = ((), (), s32[]{:S(2)}) async-start(), calls=%async_computation.23 | async-start | bytes 2211840 | tf_op jit(solution)/shard_map/all_gather | solution.py:139
  10.2 143.0 %all-gather.19.cloned.1.call-start = ((), (), s32[]{:S(2)}) async-start(), calls=%async_computation.21 | async-start | bytes 1474560 | tf_op jit(solution)/shard_map/all_gather | solution.py:142
  11.1 173.6 %all-gather.21.cloned.1.call-start = ((), (), s32[]{:S(2)}) async-start(), calls=%async_computation.22 | async-start | bytes 1474560 | tf_op jit(solution)/shard_map/all_gather | solution.py:143
  12.1 203.7 %all-gather.25.cloned.1.call-start = ((), (), s32[]{:S(2)}) async-start(), calls=%async_computation.24 | async-start | bytes 1474560 | tf_op jit(solution)/shard_map/all_gather | solution.py:142
  12.1 38.6 %copy-start.43 = (bf16[2,96,1152]{2,1,0:T(8,128)(2,1)S(1)}, bf16[2,96,1152]{2,1,0:T(8,128)(2,1)}, u32[]{:S(2)}) copy-start(bf16[2,96,1152]{2,1,0:T(8,128)(2,1)} %param.14) | copy-start | bytes 1327108
  12.7 234.7 %all-gather.27.cloned.1.call-start = ((), (), s32[]{:S(2)}) async-start(), calls=%async_computation.25 | async-start | bytes 1474560 | tf_op jit(solution)/shard_map/all_gather | solution.py:143
  13.3 365.8 %reduce-scatter.21.cloned.1.call-start = ((), (), s32[]{:S(2)}) async-start(), calls=%async_computation.15 | async-start | bytes 368640 | tf_op jit(solution)/shard_map/reduce_scatter | solution.py:169
  14.1 109.4 %copy-start.50 = (f32[4,256]{1,0:T(4,128)}, f32[4,256]{1,0:T(4,128)S(1)}, u32[]{:S(2)}) copy-start(f32[4,256]{1,0:T(4,128)S(1)} %broadcast_multiply_fusion.3) | copy-start | bytes 12292
  14.6 90.5 %copy-start.61 = (f32[4,256]{1,0:T(4,128)}, f32[4,256]{1,0:T(4,128)S(1)}, u32[]{:S(2)}) copy-start(f32[4,256]{1,0:T(4,128)S(1)} %fusion.47) | copy-start | bytes 12292
  14.6 108.9 %copy-start.69 = (f32[4,256]{1,0:T(4,128)}, f32[4,256]{1,0:T(4,128)S(1)}, u32[]{:S(2)}) copy-start(f32[4,256]{1,0:T(4,128)S(1)} %fusion.128) | copy-start | bytes 12292
  50.7 54.4 %copy-start.46 = (bf16[4,384]{1,0:T(4,128)(2,1)S(1)}, bf16[4,384]{1,0:T(4,128)(2,1)}, u32[]{:S(2)}) copy-start(bf16[4,384]{1,0:T(4,128)(2,1)} %param.10) | copy-start | bytes 9220
  105.1 18.4 %copy-start.36 = (bf16[1,384,1152]{2,1,0:T(8,128)(2,1)}, bf16[1,384,1152]{2,1,0:T(8,128)(2,1)S(1)}, u32[]{:S(2)}) copy-start(bf16[1,384,1152]{2,1,0:T(8,128)(2,1)S(1)} %all-gather.1) | copy-start | bytes 2654212
  107.3 19.3 %copy-start.52 = (f32[4,384]{1,0:T(4,128)}, f32[4,384]{1,0:T(4,128)S(1)}, u32[]{:S(2)}) copy-start(f32[4,384]{1,0:T(4,128)S(1)} %get-tuple-element.61) | copy-start | bytes 18436
  107.3 19.3 %copy-start.78 = (f32[4,384]{1,0:T(4,128)}, f32[4,384]{1,0:T(4,128)S(1)}, u32[]{:S(2)}) copy-start(f32[4,384]{1,0:T(4,128)S(1)} %get-tuple-element.60) | copy-start | bytes 18436
  107.3 45.8 %copy-start.54 = (f32[4,384]{1,0:T(4,128)}, f32[4,384]{1,0:T(4,128)S(1)}, u32[]{:S(2)}) copy-start(f32[4,384]{1,0:T(4,128)S(1)} %get-tuple-element.58) | copy-start | bytes 18436
  107.3 77.4 %copy-start.75 = (f32[4,384]{1,0:T(4,128)}, f32[4,384]{1,0:T(4,128)S(1)}, u32[]{:S(2)}) copy-start(f32[4,384]{1,0:T(4,128)S(1)} %get-tuple-element.57) | copy-start | bytes 18436
  123.5 68.1 %copy-start.57 = (f32[4,384]{1,0:T(4,128)}, f32[4,384]{1,0:T(4,128)S(1)}, u32[]{:S(2)}) copy-start(f32[4,384]{1,0:T(4,128)S(1)} %get-tuple-element.55) | copy-start | bytes 18436
  143.0 16.0 %copy-start.63 = (f32[4,256]{1,0:T(4,128)}, f32[4,256]{1,0:T(4,128)S(1)}, u32[]{:S(2)}) copy-start(f32[4,256]{1,0:T(4,128)S(1)} %multiply_reduce_fusion.16) | copy-start | bytes 12292
  247.3 7.5 %copy-start.34 = (bf16[1,384,1536]{2,1,0:T(8,128)(2,1)S(1)}, bf16[1,384,1536]{2,1,0:T(8,128)(2,1)}, u32[]{:S(2)}) copy-start(bf16[1,384,1536]{2,1,0:T(8,128)(2,1)} %all-gather.25.cloned.1.call-done) | copy-start | bytes 3538948
  260.0 6.2 copy-start.24
  272.8 5.2 copy-start.12
  272.8 5.2 copy-start.40
  272.8 11.9 %slice-start = ((s8[6291456]{0:T(1024)(128)(4,1)}), s8[4194304]{0:T(1024)(128)(4,1)S(1)}, s32[]{:S(2)}) async-start(s8[6291456]{0:T(1024)(128)(4,1)} %bitcast.220), calls=%async_computation.27 | async-start | bytes 8388608
  277.9 6.8 slice-start.1
  292.5 86.6 %reduce-scatter.19.cloned.1.call-start = ((), (), s32[]{:S(2)}) async-start(), calls=%async_computation.14 | async-start | bytes 368640 | tf_op jit(solution)/shard_map/reduce_scatter | solution.py:169
  301.5 8.8 %copy-start.16 = (f32[4,256,384]{2,1,0:T(8,128)}, f32[4,256,384]{2,1,0:T(8,128)S(1)}, u32[]{:S(2)}) copy-start(f32[4,256,384]{2,1,0:T(8,128)S(1)} %get-tuple-element.26) | copy-start | bytes 4718596
  302.1 5.3 copy-start.33
  319.5 61.3 %reduce-scatter.17.cloned.1.call-start = ((), (), s32[]{:S(2)}) async-start(), calls=%async_computation.13 | async-start | bytes 1105920 | tf_op jit(solution)/shard_map/reduce_scatter | solution.py:166
  319.6 7.2 %copy-start.5 = (f32[4,256,384]{2,1,0:T(8,128)S(1)}, f32[4,256,384]{2,1,0:T(8,128)}, u32[]{:S(2)}) copy-start(f32[4,256,384]{2,1,0:T(8,128)} %copy-done.2) | copy-start | bytes 4718596
  319.6 7.2 %copy-start.28 = (bf16[4,256,3,6,64]{1,4,3,2,0:T(8,128)(2,1)S(1)}, bf16[4,256,3,6,64]{1,4,3,2,0:T(8,128)(2,1)}, u32[]{:S(2)}) copy-start(bf16[4,256,3,6,64]{1,4,3,2,0:T(8,128)(2,1)} %copy-done.27) | copy-start | bytes 7077892
  319.6 7.2 %copy-start.83 = (f32[4,384]{1,0:T(4,128)S(1)}, f32[4,384]{1,0:T(4,128)}, u32[]{:S(2)}) copy-start(f32[4,384]{1,0:T(4,128)} %get-tuple-element.54) | copy-start | bytes 18436
  329.4 60.4 %reduce-scatter.15.cloned.1.call-start = ((), (), s32[]{:S(2)}) async-start(), calls=%async_computation.12 | async-start | bytes 1105920 | tf_op jit(solution)/shard_map/reduce_scatter | solution.py:166
  329.6 6.3 copy-start.11
  346.6 7.0 copy-start.77
  346.6 73.7 %reduce-scatter.29.cloned.1.call-start = ((), (), s32[]{:S(2)}) async-start(), calls=%async_computation.19 | async-start | bytes 1474560 | tf_op jit(solution)/shard_map/reduce_scatter | solution.py:175
  353.5 7.2 %copy-start.56 = (f32[4,384]{1,0:T(4,128)S(1)}, f32[4,384]{1,0:T(4,128)}, u32[]{:S(2)}) copy-start(f32[4,384]{1,0:T(4,128)} %get-tuple-element.52) | copy-start | bytes 18436
  353.5 96.9 %reduce-scatter.27.cloned.1.call-start = ((), (), s32[]{:S(2)}) async-start(), calls=%async_computation.18 | async-start | bytes 1474560 | tf_op jit(solution)/shard_map/reduce_scatter | solution.py:175
  360.7 4.9 copy-start.55
  360.7 120.5 %reduce-scatter.25.cloned.1.call-start = ((), (), s32[]{:S(2)}) async-start(), calls=%async_computation.17 | async-start | bytes 1474560 | tf_op jit(solution)/shard_map/reduce_scatter | solution.py:172
  365.3 5.0 copy-start.72
  365.3 5.0 copy-start.71
  365.3 5.0 copy-start.84
  365.3 5.0 copy-start.47
  365.3 146.6 %reduce-scatter.23.cloned.1.call-start = ((), (), s32[]{:S(2)}) async-start(), calls=%async_computation.16 | async-start | bytes 1474560 | tf_op jit(solution)/shard_map/reduce_scatter | solution.py:172
  370.1 181.6 %reduce-scatter.13.cloned.1.call-start = ((), (), s32[]{:S(2)}) async-start(), calls=%async_computation.11 | async-start | bytes 2211840 | tf_op jit(solution)/shard_map/reduce_scatter | solution.py:163
  372.3 219.3 %reduce-scatter.11.cloned.1.call-start = ((), (), s32[]{:S(2)}) async-start(), calls=%async_computation.10 | async-start | bytes 2211840 | tf_op jit(solution)/shard_map/reduce_scatter | solution.py:163
  379.0 310.3 %all-reduce.3.cloned.1.call-start = ((), (), s32[]{:S(2)}) async-start(), calls=%async_computation.26 | async-start | bytes 10616832 | tf_op jit(solution)/shard_map/psum | solution.py:183
  (65 other events, 172.0 us)
Sparse Core Ops, SparseCore 0:
  10.2 58.5 all-gather.16
  70.9 50.1 all-gather.22
  123.3 29.8 all-gather.18
  155.2 29.5 all-gather.20
  186.2 29.5 all-gather.24
  217.8 29.5 all-gather.26
  292.6 18.9 reduce-scatter.20
  319.7 18.9 reduce-scatter.18
  341.0 22.8 reduce-scatter.16
  366.1 23.6 reduce-scatter.14
  392.1 28.1 reduce-scatter.28
  422.5 27.8 reduce-scatter.26
  453.3 27.8 reduce-scatter.24
  484.0 27.8 reduce-scatter.22
  514.6 37.0 reduce-scatter.12
  554.1 37.4 reduce-scatter.10
  595.9 93.4 all-reduce.2
where the time goes:
time: 714 us; the launch traced here: 703 us
  waiting for transfers between devices  373 us (52%)
  matrix products  141 us (20%)
  blocking collectives  90.4 us (13%)
  other arithmetic  45.5 us (6%)
  local copies, waits for them, and re-layouts  37 us (5%)
  between operations  15.6 us (2%)
    psum x1, waiting for transfers between devices, body(): lax.psum((stacked[0], stacked[1], stacked[2], stacked[3], stacked[4]), 'dp')  89.1 us
    reduce_scatter x2, waiting for transfers between devices, body(): lax.psum_scatter(g_ada.astype(jnp.bfloat16), 'fsdp', scatter_dimension=0,...  77.5 us
    reduce_scatter x2, waiting for transfers between devices, body(): lax.psum_scatter(g_up.astype(jnp.bfloat16), 'fsdp', scatter_dimension=0,...  59.3 us
    reduce_scatter x2, waiting for transfers between devices, body(): lax.psum_scatter(g_down.astype(jnp.bfloat16), 'fsdp', scatter_dimension=0...  58.6 us
    all_gather x2, blocking collectives, body(): lax.all_gather(w_qkv[index], 'fsdp', axis=0, tiled=True)  54.4 us
    all_gather x2, waiting for transfers between devices, body(): lax.all_gather(w_down[index], 'fsdp', axis=0, tiled=True)  51.6 us
    all_gather x2, blocking collectives, body(): lax.all_gather(w_proj[index], 'fsdp', axis=0, tiled=True)  36.1 us
    unnamed x207, local copies, waits for them, and re-layouts  19.3 us
  transfers between devices with their start and end apart: 17, of which 13 were waited for; matrix products, arithmetic and copies ran while one was open for 22% of the time, Pallas kernels for 0%

commit v1 on v0

v1 whole, which is shorter than its diff:
```python
import functools

import jax
import jax.numpy as jnp
from jax import lax
from jax.experimental import pallas as pl
from jax.experimental.pallas import tpu as pltpu
from jax.sharding import PartitionSpec as P

MESH = pl.DeviceIdType.MESH
bf, f32 = jnp.bfloat16, jnp.float32
HEADS = 6
GROUP = 8
NN = (((1,), (0,)), ((), ()))
NT = (((1,), (1,)), ((), ()))
TN = (((0,), (0,)), ((), ()))
GELU_A = 0.7978845608028654
GELU_B = GELU_A * 0.044715


def dot(a, b, dims=NN):
    return lax.dot_general(a, b, dims, preferred_element_type=f32)


def exact_dot(a, b, dims=NN):
    return lax.dot_general(a, b, dims, precision=lax.Precision.HIGHEST, preferred_element_type=f32)


def one_hot(shape, hit):
    r = lax.broadcasted_iota(jnp.int32, shape, 0)
    c = lax.broadcasted_iota(jnp.int32, shape, 1)
    return jnp.where(hit(r, c), 1.0, 0.0)


def norm_hat(v):
    c = v - jnp.mean(v, -1, keepdims=True)
    r = lax.rsqrt(jnp.mean(c * c, -1, keepdims=True) + 1e-6)
    return c * r, r


def norm_back(dx, hat, r):
    return r * (dx - jnp.mean(dx, -1, keepdims=True) - hat * jnp.mean(dx * hat, -1, keepdims=True))


class Refs:
    pass


def scratch(F, I, L, D, FF, B):
    T = I * L
    R = D // F // 2
    return dict(
        wq=((B, F, 2, R, FF), bf),
        wu=((B, F, 2, R, FF), bf),
        wd=((B, F, 4, 2, R, D), bf),
        wa=((B, D // F, 6 * D), bf),
        tk=((T, D), bf),
        x1=((T, D), f32),
        fi=((B, T, D), bf),
        qkv=((B, T, 3 * D), bf),
        pt=((B, I * HEADS, L, L), bf),
        mt=((B, D, T), bf),
        att=((B, T, D), bf),
        mid=((B, T, D), f32),
        si=((B, T, D), bf),
        hid=((B, T, FF), bf),
        br=((B, T, D), bf),
        g=((T, D), f32),
        db=((T, D), bf),
        act=((T, FF), bf),
        da=((T, D), bf),
        os=((T, D), bf),
        mod=((B, 6 * I, D), f32),
        dm=((B, 32, D), f32),
        cd=((I, D), bf),
        gc=((8, D), f32),
        ms=((B, F, 24, D), f32),
        mr=((B, F, 24, D), f32),
        cg=((4, 2, F, 16, D), bf),
        dg=((B, 2, 4, 2, F, 16, D), bf),
        cs=((F, 8, D), f32),
        cr=((F, 8, D), f32),
        gq=((F, 2, R, FF), bf),
        gu=((F, 2, R, FF), bf),
        gd=((F, 4, 2, R, D), bf),
        hq=((B, F, R, FF), bf),
        hu=((B, F, R, FF), bf),
        hd=((B, F, 4, R, D), bf),
        qr=((B, 3, 3, F, R, D), bf),
        qs=((B, 3, F, R, D), bf),
        zr=((B, 3, F, R, D), bf),
        oq=((B, 2, R, FF), bf),
        ou=((B, 2, R, FF), bf),
        od=((B, 4, 2, R, D), bf),
    )


INPUTS = ("tokens", "cond", "cotangent", "mask", "ada", "qkv_w", "proj_w", "up_w", "down_w")
OUTPUTS = ("output", "grad_tokens", "grad_cond", "grad_ada", "grad_q", "grad_u", "grad_d")
N_SEMS = 256


def kernel(names, F, I, L, D, FF, B, *refs):
    n_in, n_out = len(INPUTS), len(OUTPUTS)
    inp, out, k = Refs(), Refs(), Refs()
    for name, ref in zip(INPUTS, refs[:n_in]):
        setattr(inp, name, ref)
    for name, ref in zip(OUTPUTS, refs[n_in : n_in + n_out]):
        setattr(out, name, ref)
    for name, ref in zip(names, refs[n_in + n_out :]):
        setattr(k, name, ref)
    sems, local_sems = refs[-2], refs[-1]
    R = D // F // 2
    HS = D // HEADS
    KINDS = ("q", "u", "d")

    me, f = lax.axis_index("dp"), lax.axis_index("fsdp")
    e = me % GROUP
    base = me - e
    c, q = e % 2, e // 2
    other = 1 - c
    z_peer = [(f + r) % F for r in range(F)]
    q_peer = [(q + j) % 4 for j in range(4)]

    def at_z(r):
        return (me, z_peer[r])

    def at_q(j):
        return (base + 2 * q_peer[j] + c, f)

    at_c = (base + 2 * q + other, f)

    def rows(i, n=L):
        return pl.ds(pl.multiple_of(i * n, n), n)

    def quarter(j):
        return pl.ds(pl.multiple_of(q_peer[j] * D, D), D)

    index = {}

    def sem(key):
        return sems.at[index.setdefault(key, len(index))]

    pending = []

    def send(key, src, dst, to):
        pltpu.make_async_remote_copy(
            src_ref=src,
            dst_ref=dst,
            send_sem=sem(("send",) + key),
            recv_sem=sem(("recv",) + key),
            device_id=to,
            device_id_type=MESH,
        ).start()

    def wait(kind, key, like):
        pltpu.make_async_copy(like, like, sem((kind,) + key)).wait()

    local_index = {}

    def local(key, src, dst):
        copy = pltpu.make_async_copy(
            src, dst, local_sems.at[local_index.setdefault(key, len(local_index))]
        )
        return copy

    whole = {"q": k.wq, "u": k.wu, "d": k.wd}

    def w_piece(b, w, fz, qi, ci):
        if w == "d":
            return k.wd.at[b, fz, qi, ci]
        return whole[w].at[b, fz, ci, :, pl.ds(pl.multiple_of(qi * D, D), D)]

    def w_half(b, w, fz, ci):
        if w == "d":
            return k.wd.at[b, fz, :, ci]
        return whole[w].at[b, fz, ci]

    def w_like(b, w, n):
        if w == "d":
            return k.wd.at[b, pl.ds(0, n // 3), pl.ds(0, 3), 0] if n % 3 == 0 else k.wd.at[b, 0, pl.ds(0, n), 0]
        return whole[w].at[b, pl.ds(0, n // 3), 0, :, pl.ds(0, 3 * D)] if n % 3 == 0 else whole[w].at[b, 0, 0, :, pl.ds(0, n * D)]

    def w_z(b, w):
        for r in range(1, F):
            send(("wz", b, w), w_piece(b, w, f, q, c), w_piece(b, w, f, q, c), at_z(r))

    def w_zq(b, w):
        wait("recv", ("wz", b, w), w_like(b, w, F - 1))
        for j in range(1, 4):
            for r in range(1, F):
                p = w_piece(b, w, z_peer[r], q, c)
                send(("wq", b, w), p, p, at_q(j))

    def w_qc(b, w):
        wait("recv", ("wq", b, w), w_like(b, w, 3 * (F - 1)))
        for r in range(1, F):
            p = w_half(b, w, z_peer[r], c)
            send(("wc", b, w), p, p, at_c)

    def w_ready(b, w):
        wait("recv", ("wc", b, w), w_like_halves(b, w))

    def w_like_halves(b, w):
        return k.wd.at[b, pl.ds(0, F - 1), :, 0] if w == "d" else whole[w].at[b, pl.ds(0, F - 1), 0]

    def w_sent():
        for b in range(B):
            for w in KINDS:
                wait("send", ("wz", b, w), w_like(b, w, F - 1))
                wait("send", ("wq", b, w), w_like(b, w, 3 * (F - 1)))
                wait("send", ("wc", b, w), w_like_halves(b, w))

    def cols():
        return one_hot((D, D // F), lambda r, s: r == f * (D // F) + s)

    def cond_start():
        v = k.cd[...].astype(f32)
        a = v / (1.0 + jnp.exp(-v))
        k.cg[q, c, f] = jnp.concatenate([a] * 4, axis=0).astype(bf)
        for r in range(1, F):
            send(("cz",), k.cg.at[q, c, f], k.cg.at[q, c, f], at_z(r))

    def cond_zq():
        for j in range(1, 4):
            send(("cq",), k.cg.at[q, c], k.cg.at[q, c], at_q(j))

    def cond_qc():
        wait("recv", ("cq",), k.cg.at[pl.ds(0, 3), 0])
        send(("cc",), k.cg.at[:, c], k.cg.at[:, c], at_c)

    def cond_ready():
        wait("recv", ("cc",), k.cg.at[:, 0])

    def tile_mask(n, p):
        r = lax.broadcasted_iota(jnp.int32, (n, 1), 0)
        return jnp.where((r // 4) % 4 == p, 1.0, 0.0)

    def mod_partial(b):
        a = dot(k.cg[q, c].reshape(F * 16, D), cols().astype(bf))
        lo, hi = (a * tile_mask(F * 16, 0)).astype(bf), (a * tile_mask(F * 16, 1)).astype(bf)
        for s in range(3):
            t = dot(lo, k.wa[b, :, 2 * s * D : (2 * s + 1) * D]) + dot(hi, k.wa[b, :, (2 * s + 1) * D : (2 * s + 2) * D])
            k.ms[b, :, 8 * s : 8 * s + 8, :] = t.reshape(F, 16, D)[:, :8]
        for r in range(1, F):
            send(("mz", b), k.ms.at[b, z_peer[r]], k.mr.at[b, f], at_z(r))

    def mod_ready(b):
        wait("recv", ("mz", b), k.mr.at[b, pl.ds(0, F - 1)])
        total = k.ms[b, f]
        for r in range(1, F):
            total = total + k.mr[b, z_peer[r]]
        k.mod[b] = total

    def piece(b, i, p):
        return k.mod[b, pl.ds(p * I + i, 1), :]

    def dm_row(b, i, p, v):
        at = (p - 2) * I if p >= 2 else 16 + p * I
        k.dm[b, pl.ds(at + i, 1), :] = v

    def dm_start(b, late):
        k.dg[b, late, q, c, f] = k.dm[b, 16 * late : 16 * late + 16].astype(bf)
        for r in range(1, F):
            p = k.dg.at[b, late, q, c, f]
            send(("dz", b, late), p, p, at_z(r))

    def dm_zq(b, late):
        wait("recv", ("dz", b, late), k.dg.at[b, late, 0, 0, pl.ds(0, F - 1)])
        for j in range(1, 4):
            p = k.dg.at[b, late, q, c]
            send(("dq", b, late), p, p, at_q(j))

    def dm_qc(b, late):
        wait("recv", ("dq", b, late), k.dg.at[b, late, pl.ds(0, 3), 0])
        p = k.dg.at[b, late, :, c]
        send(("dc", b, late), p, p, at_c)

    def dm_ready(b, late):
        wait("recv", ("dc", b, late), k.dg.at[b, late, :, 0])

    def dcond_part(b, late):
        t = k.dg[b, late, q, c].reshape(F * 16, D).astype(f32)
        acc = None
        for p in range(2 if late else 4):
            at = (p if late else p + 2) * D
            o = dot((t * tile_mask(F * 16, p)).astype(bf), k.wa[b, :, at : at + D], NT)
            acc = o if acc is None else acc + o
        return acc

    def dcond_send():
        acc = dcond_part(0, 0) + dcond_part(0, 1) + dcond_part(1, 0) + dcond_part(1, 1)
        fold = one_hot((F * 8, F * 16), lambda r, s: (r // 8 == s // 16) & (r % 8 == s % 4))
        t = exact_dot(exact_dot(fold, acc), cols(), NT)
        k.cs[...] = t.reshape(F, 8, D)
        for r in range(1, F):
            send(("gz",), k.cs.at[z_peer[r]], k.cr.at[f], at_z(r))

    def dcond_finish():
        wait("recv", ("gz",), k.cr.at[pl.ds(0, F - 1)])
        total = k.cs[f]
        for r in range(1, F):
            total = total + k.cr[z_peer[r]]
        v = k.cd[...].astype(f32)
        s = 1.0 / (1.0 + jnp.exp(-v))
        k.gc[:I] = total[:I] * (s * (1.0 + v * (1.0 - s)))
        local(("grad_cond",), k.gc.at[pl.ds(0, I)], out.grad_cond).start()

    def grad_ada(b, late):
        n = GROUP * F * 16
        a = dot(k.cg[...].reshape(n, D), cols().astype(bf))
        t = k.dg[b, late].reshape(n, D)
        stage = (k.mid.at[1], k.x1)[b]
        for p in range(2 if late else 4):
            m = p if late else p + 2
            at = pl.ds(m * (D // F), D // F)
            stage[at, :] = dot((a * tile_mask(n, p)).astype(bf), t, TN)
            local(("ada", b, m), stage.at[at], out.grad_ada.at[b, :, pl.ds(m * D, D)]).start()

    grads = {"q": k.gq, "u": k.gu, "d": k.gd}
    halves = {"q": k.hq, "u": k.hu, "d": k.hd}
    results = {"q": k.oq, "u": k.ou, "d": k.od}
    outs = {"q": out.grad_q, "u": out.grad_u, "d": out.grad_d}
    number = {"q": 0, "u": 1, "d": 2}

    def g_half(w, ci):
        return grads[w].at[:, :, ci] if w == "d" else grads[w].at[:, ci]

    def h_quarter(b, w, j):
        return k.hd.at[b, :, q_peer[j]] if w == "d" else halves[w].at[b, :, :, quarter(j)]

    def r_piece(b, w):
        return k.od.at[b, q, c] if w == "d" else results[w].at[b, c, :, quarter(0)]

    def r_half(b, w, ci):
        return k.od.at[b, :, ci] if w == "d" else results[w].at[b, ci]

    def g_c(b, w):
        send(("gc", b, w), g_half(w, other), halves[w].at[b], at_c)

    def g_cq(b, w):
        wait("recv", ("gc", b, w), halves[w].at[b])
        wait("send", ("gc", b, w), halves[w].at[b])

        def add(n, _):
            own = k.gd[n, :, c] if w == "d" else grads[w][n, c]
            halves[w][b, n] = (halves[w][b, n].astype(f32) + own.astype(f32)).astype(bf)
            return 0

        lax.fori_loop(0, F, add, 0)
        for j in range(1, 4):
            send(("gq", b, w), h_quarter(b, w, j), k.qr.at[b, number[w], j - 1], at_q(j))

    def g_qz(b, w):
        m = number[w]
        wait("recv", ("gq", b, w), k.qr.at[b, m])

        def add(n, _):
            own = k.hd[b, n, q] if w == "d" else halves[w][b, n, :, quarter(0)]
            total = own.astype(f32)
            for j in range(3):
                total = total + k.qr[b, m, j, n].astype(f32)
            k.qs[b, m, n] = total.astype(bf)
            return 0

        lax.fori_loop(0, F, add, 0)
        for r in range(1, F):
            send(("gz", b, w), k.qs.at[b, m, z_peer[r]], k.zr.at[b, m, f], at_z(r))

    def g_zq(b, w):
        m = number[w]
        wait("recv", ("gz", b, w), k.zr.at[b, m, pl.ds(0, F - 1)])
        total = k.qs[b, m, f].astype(f32)
        for r in range(1, F):
            total = total + k.zr[b, m, z_peer[r]].astype(f32)
        total = total.astype(bf)
        if w == "d":
            k.od[b, q, c] = total
        else:
            results[w][b, c, :, quarter(0)] = total
        for j in range(1, 4):
            send(("rq", b, w), r_piece(b, w), r_piece(b, w), at_q(j))

    def g_qc(b, w):
        wait("recv", ("rq", b, w), k.qr.at[b, number[w], 0, pl.ds(0, 3)])
        send(("rc", b, w), r_half(b, w, c), r_half(b, w, c), at_c)

    def g_done(b, w):
        wait("recv", ("rc", b, w), r_half(b, w, 0))
        local(("out", b, w), results[w].at[b], outs[w].at[b]).start()

    def rest_sent():
        wait("send", ("cz",), k.cg.at[0, 0, pl.ds(0, F - 1)])
        wait("send", ("cq",), k.cg.at[pl.ds(0, 3), 0])
        wait("send", ("cc",), k.cg.at[:, 0])
        wait("send", ("gz",), k.cs.at[pl.ds(0, F - 1)])
        for b in range(B):
            wait("send", ("mz", b), k.ms.at[b, pl.ds(0, F - 1)])
            for late in range(2):
                wait("send", ("dz", b, late), k.dg.at[b, late, 0, 0, pl.ds(0, F - 1)])
                wait("send", ("dq", b, late), k.dg.at[b, late, pl.ds(0, 3), 0])
                wait("send", ("dc", b, late), k.dg.at[b, late, :, 0])
            for w in KINDS:
                m = number[w]
                wait("send", ("gq", b, w), k.qr.at[b, m])
                wait("send", ("gz", b, w), k.zr.at[b, m, pl.ds(0, F - 1)])
                wait("send", ("rq", b, w), k.qr.at[b, m, 0, pl.ds(0, 3)])
                wait("send", ("rc", b, w), r_half(b, w, 0))

    def m_qkv(b):
        return k.wq[b, :, :, :, : 3 * D].reshape(D, 3 * D)

    def m_proj(b):
        return k.wq[b, :, :, :, 3 * D :].reshape(D, D)

    def m_up(b, at, n):
        return k.wu[b, :, :, :, at : at + n].reshape(D, n)

    def m_down(b):
        return k.wd[b].reshape(FF, D)

    def state(b, r):
        return k.tk[r, :].astype(f32) if b == 0 else k.x1[r, :]

    def lane_masks():
        lane = lax.broadcasted_iota(jnp.int32, (1, 2 * HS), 1)
        lo = jnp.where(lane < HS, 1.0, 0.0)
        return lo.astype(bf), (1.0 - lo).astype(bf)

    def fwd_attention(b, i):
        r = rows(i)
        x = state(b, r)
        hat, _ = norm_hat(x)
        first = (hat * (1.0 + piece(b, i, 1)) + piece(b, i, 0)).astype(bf)
        k.fi[b, r, :] = first
        qkv = dot(first, m_qkv(b))
        qs = (qkv[:, :D] * HS**-0.5).astype(bf)
        ks = qkv[:, D : 2 * D].astype(bf)
        vs = qkv[:, 2 * D :].astype(bf)
        k.qkv[b, r, :D] = qs
        k.qkv[b, r, D : 2 * D] = ks
        k.qkv[b, r, 2 * D :] = vs
        vt = vs.T
        masks = lane_masks()
        mixed = []
        for h in range(HEADS):
            s = slice((h // 2) * 2 * HS, (h // 2 + 1) * 2 * HS)
            scores = dot(ks[:, s] * masks[h % 2], qs[:, s], NT)
            ex = jnp.exp(scores - jnp.max(scores, axis=0, keepdims=True))
            probs = (ex * (1.0 / jnp.sum(ex, axis=0, keepdims=True))).astype(bf)
            k.pt[b, i * HEADS + h] = probs
            mixed.append(dot(vt[h * HS : (h + 1) * HS], probs))
        mt = jnp.concatenate(mixed, axis=0).astype(bf)
        k.mt[b, :, r] = mt
        att = dot(mt, m_proj(b), TN)
        k.att[b, r, :] = att.astype(bf)
        mid = x + piece(b, i, 2) * att
        k.mid[b, r, :] = mid
        hat, _ = norm_hat(mid)
        k.si[b, r, :] = (hat * (1.0 + piece(b, i, 4)) + piece(b, i, 3)).astype(bf)

    def fwd_mlp(b, i):
        r = rows(i)
        second = k.si[b, r, :]
        n = FF // 3
        acc = None
        for j in range(3):
            x = dot(second, m_up(b, j * n, n))
            k.hid[b, r, j * n : (j + 1) * n] = x.astype(bf)
            a = (x * (0.5 * jnp.tanh(x * (GELU_A + GELU_B * (x * x))) + 0.5)).astype(bf)
            o = dot(a, m_down(b)[j * n : (j + 1) * n])
            acc = o if acc is None else acc + o
        k.br[b, r, :] = acc.astype(bf)
        y = k.mid[b, r, :] + piece(b, i, 5) * acc
        if b < B - 1:
            k.x1[r, :] = y
        else:
            k.os[r, :] = y.astype(bf)
            k.g[r, :] = k.db[r, :].astype(f32) * inp.mask[i].astype(f32)

    def bwd_mlp(b, i):
        r = rows(i)
        g = k.g[r, :]
        dm_row(b, i, 5, jnp.sum(g * k.br[b, r, :].astype(f32), axis=0, keepdims=True))
        db = (g * piece(b, i, 5)).astype(bf)
        k.db[r, :] = db
        n = FF // 3
        acc = None
        for j in range(3):
            s = slice(j * n, (j + 1) * n)
            da = dot(db, m_down(b)[s], NT)
            x = k.hid[b, r, s].astype(f32)
            x2 = x * x
            t = jnp.tanh(x * (GELU_A + GELU_B * x2))
            h = 0.5 * t + 0.5
            a = x * h
            k.act[r, s] = a.astype(bf)
            dh = ((a * (1.0 - t) * (GELU_A + (3 * GELU_B) * x2) + h) * da).astype(bf)
            k.hid[b, r, s] = dh
            o = dot(dh, m_up(b, j * n, n), NT)
            acc = o if acc is None else acc + o
        hat, rs = norm_hat(k.mid[b, r, :])
        dm_row(b, i, 3, jnp.sum(acc, axis=0, keepdims=True))
        dm_row(b, i, 4, jnp.sum(acc * hat, axis=0, keepdims=True))
        d_mid = g + norm_back(acc * (1.0 + piece(b, i, 4)), hat, rs)
        k.g[r, :] = d_mid
        dm_row(b, i, 2, jnp.sum(d_mid * k.att[b, r, :].astype(f32), axis=0, keepdims=True))
        k.da[r, :] = (d_mid * piece(b, i, 2)).astype(bf)

    def grad_down(b):
        k.gd[...] = dot(k.act[...], k.db[...], TN).astype(bf).reshape(F, 4, 2, R, D)

    def grad_up(b):
        k.gu[...] = dot(k.si[b], k.hid[b], TN).astype(bf).reshape(F, 2, R, FF)

    def grad_proj(b):
        k.gq[:, :, :, 3 * D :] = dot(k.mt[b], k.da[...]).astype(bf).reshape(F, 2, R, D)

    def grad_qkv(b):
        k.gq[:, :, :, : 3 * D] = dot(k.fi[b], k.qkv[b], TN).astype(bf).reshape(F, 2, R, 3 * D)

    def bwd_attention(b, i):
        r = rows(i)
        do = dot(k.da[r, :], m_proj(b), NT).astype(bf)
        qs = k.qkv[b, r, :D]
        ks = k.qkv[b, r, D : 2 * D]
        vs = k.qkv[b, r, 2 * D :]
        kt = ks.T
        masks = lane_masks()
        dq = []
        for p in range(HEADS // 2):
            s = slice(p * 2 * HS, (p + 1) * 2 * HS)
            dv = dk = None
            for m in range(2):
                h = 2 * p + m
                probs = k.pt[b, i * HEADS + h]
                dp = dot(vs[:, s] * masks[m], do[:, s], NT)
                pf = probs.astype(f32)
                w = pf * dp
                ds = (w - pf * jnp.sum(w, axis=0, keepdims=True)).astype(bf)
                o = dot(probs, do[:, s] * masks[m])
                dv = o if dv is None else dv + o
                o = dot(ds, qs[:, s] * masks[m])
                dk = o if dk is None else dk + o
                dq.append(dot(kt[h * HS : (h + 1) * HS], ds))
            k.qkv[b, r, D + p * 2 * HS : D + (p + 1) * 2 * HS] = dk.astype(bf)
            k.qkv[b, r, 2 * D + p * 2 * HS : 2 * D + (p + 1) * 2 * HS] = dv.astype(bf)
        k.qkv[b, r, :D] = (jnp.concatenate(dq, axis=0) * HS**-0.5).astype(bf).T

    def bwd_first(b, i):
        r = rows(i)
        acc = dot(k.qkv[b, r, :], m_qkv(b), NT)
        hat, rs = norm_hat(state(b, r))
        dm_row(b, i, 0, jnp.sum(acc, axis=0, keepdims=True))
        dm_row(b, i, 1, jnp.sum(acc * hat, axis=0, keepdims=True))
        k.g[r, :] = k.g[r, :] + norm_back(acc * (1.0 + piece(b, i, 1)), hat, rs)

    def images(fn, b, tasks={}):
        def step(i, _):
            for at, todo in tasks.items():
                pl.when(i == at)(functools.partial(run, todo))
            fn(b, i)
            return 0

        lax.fori_loop(0, I, step, 0)

    def run(todo):
        for fn, *args in todo:
            fn(*args)

    loads = [
        local(("cd",), inp.cond, k.cd),
        local(("wa",), inp.ada, k.wa),
        local(("wq",), inp.qkv_w, k.wq.at[:, f, :, :, pl.ds(0, 3 * D)]),
        local(("wp",), inp.proj_w, k.wq.at[:, f, :, :, pl.ds(3 * D, D)]),
        local(("tk",), inp.tokens, k.tk),
        local(("wu",), inp.up_w, k.wu.at[:, f]),
        local(("wd",), inp.down_w, k.wd.at[:, f]),
        local(("db",), inp.cotangent, k.db),
    ]
    for copy in loads:
        copy.start()
    k.dm[...] = jnp.zeros_like(k.dm)

    barrier = pltpu.get_barrier_semaphore()
    everyone = [at_z(r) for r in range(1, F)] + [at_q(j) for j in range(1, 4)] + [at_c]
    for peer in everyone:
        pl.semaphore_signal(barrier, inc=1, device_id=peer, device_id_type=MESH)
    pl.semaphore_wait(barrier, len(everyone))

    for copy in loads:
        copy.wait()
    cond_start()
    w_z(0, "q")
    wait("recv", ("cz",), k.cg.at[0, 0, pl.ds(0, F - 1)])
    mod_partial(0)
    w_z(0, "u")
    w_z(0, "d")
    w_zq(0, "q")
    mod_partial(1)
    w_z(1, "q")
    mod_ready(0)
    w_zq(0, "u")
    w_qc(0, "q")
    w_zq(0, "d")
    w_ready(0, "q")
    images(
        fwd_attention,
        0,
        {
            0: [(w_z, 1, "u"), (w_z, 1, "d"), (cond_zq,)],
            1: [(w_qc, 0, "u"), (w_zq, 1, "q")],
            2: [(mod_ready, 1), (w_zq, 1, "u")],
            3: [(w_qc, 0, "d"), (cond_qc,), (w_zq, 1, "d")],
        },
    )
    run([(w_ready, 0, "u"), (w_ready, 0, "d")])
    images(fwd_mlp, 0, {0: [(w_qc, 1, "q")], 2: [(cond_ready,)]})
    w_ready(1, "q")
    images(fwd_attention, 1, {1: [(w_qc, 1, "u")], 3: [(w_qc, 1, "d")]})
    run([(w_ready, 1, "u"), (w_ready, 1, "d")])
    images(fwd_mlp, 1)
    local(("os",), k.os, out.output).start()

    images(bwd_mlp, 1)
    grad_down(1)
    g_c(1, "d")
    dm_start(1, 0)
    grad_up(1)
    g_c(1, "u")
    grad_proj(1)
    images(bwd_attention, 1, {0: [(g_cq, 1, "d")], 1: [(g_cq, 1, "u"), (dm_zq, 1, 0)]})
    grad_qkv(1)
    g_c(1, "q")
    images(bwd_first, 1, {1: [(g_qz, 1, "d")], 2: [(g_cq, 1, "q")], 3: [(dm_qc, 1, 0)]})
    dm_start(1, 1)
    images(
        bwd_mlp,
        0,
        {
            0: [(g_zq, 1, "d"), (dm_ready, 1, 0)],
            1: [(g_qz, 1, "u"), (dm_zq, 1, 1)],
            2: [(g_qc, 1, "d")],
            3: [(g_zq, 1, "u")],
        },
    )
    grad_down(0)
    g_c(0, "d")
    dm_start(0, 0)
    grad_up(0)
    g_c(0, "u")
    grad_proj(0)
    images(
        bwd_attention,
        0,
        {
            0: [(g_cq, 0, "d"), (g_qz, 1, "q"), (g_done, 1, "d"), (dm_qc, 1, 1)],
            1: [(g_cq, 0, "u"), (g_qc, 1, "u"), (dm_zq, 0, 0), (dm_ready, 1, 1), (grad_ada, 1, 0)],
            2: [(g_zq, 1, "q"), (g_done, 1, "u"), (grad_ada, 1, 1)],
            3: [(dm_qc, 0, 0)],
        },
    )
    grad_qkv(0)
    g_c(0, "q")
    images(
        bwd_first,
        0,
        {0: [(g_qc, 1, "q")], 1: [(g_qz, 0, "d")], 2: [(g_cq, 0, "q"), (dm_ready, 0, 0)], 3: [(g_done, 1, "q")]},
    )
    local(("g",), k.g, out.grad_tokens).start()
    dm_start(0, 1)
    run(
        [
            (grad_ada, 0, 0),
            (g_zq, 0, "d"),
            (dm_zq, 0, 1),
            (dcond_send,),
            (g_qz, 0, "u"),
            (g_qc, 0, "d"),
            (dm_qc, 0, 1),
            (dcond_finish,),
            (g_zq, 0, "u"),
            (g_done, 0, "d"),
            (dm_ready, 0, 1),
            (grad_ada, 0, 1),
            (g_qz, 0, "q"),
            (g_qc, 0, "u"),
            (g_done, 0, "u"),
            (g_zq, 0, "q"),
            (g_qc, 0, "q"),
            (g_done, 0, "q"),
        ]
    )
    w_sent()
    rest_sent()
    local(("os",), k.os, out.output).wait()
    local(("g",), k.g, out.grad_tokens).wait()
    local(("grad_cond",), k.gc.at[pl.ds(0, I)], out.grad_cond).wait()
    for b in range(B):
        stage = (k.mid.at[1], k.x1)[b]
        for m in range(6):
            at = pl.ds(m * (D // F), D // F)
            local(("ada", b, m), stage.at[at], out.grad_ada.at[b, :, pl.ds(m * D, D)]).wait()
        for w in KINDS:
            local(("out", b, w), results[w].at[b], outs[w].at[b]).wait()
    assert len(index) <= N_SEMS and len(local_index) <= 64


def body(F, tokens, cond, cotangent, keep_mask, w_ada, w_qkv, w_proj, w_up, w_down):
    I, L, D = tokens.shape
    B, _, FF = w_up.shape
    R = D // F // 2
    shapes = scratch(F, I, L, D, FF, B)
    names = tuple(shapes)
    anywhere = pl.BlockSpec(memory_space=pl.ANY)
    results = pl.pallas_call(
        functools.partial(kernel, names, F, I, L, D, FF, B),
        name="blocks",
        out_shape=[
            jax.ShapeDtypeStruct((I * L, D), bf),
            jax.ShapeDtypeStruct((I * L, D), f32),
            jax.ShapeDtypeStruct((I, D), f32),
            jax.ShapeDtypeStruct((B, D // F, 6 * D), f32),
            jax.ShapeDtypeStruct((B, 2, R, FF), bf),
            jax.ShapeDtypeStruct((B, 2, R, FF), bf),
            jax.ShapeDtypeStruct((B, 4, 2, R, D), bf),
        ],
        in_specs=[pl.BlockSpec(memory_space=pltpu.SMEM) if n == "mask" else anywhere for n in INPUTS],
        out_specs=[anywhere] * len(OUTPUTS),
        scratch_shapes=[pltpu.VMEM(*shapes[n]) for n in names]
        + [pltpu.SemaphoreType.DMA((N_SEMS,)), pltpu.SemaphoreType.DMA((64,))],
        compiler_params=pltpu.CompilerParams(
            collective_id=0, has_side_effects=True, vmem_limit_bytes=64 * 2**20 - 2**17
        ),
    )(
        tokens.reshape(I * L, D),
        cond,
        cotangent.reshape(I * L, D),
        keep_mask,
        w_ada,
        w_qkv.reshape(B, 2, R, 3 * D),
        w_proj.reshape(B, 2, R, D),
        w_up.reshape(B, 2, R, FF),
        w_down.reshape(B, 4, 2, R, D),
    )
    output, grad_tokens, grad_cond, grad_ada, grad_q, grad_u, grad_d = results
    grad_q = grad_q.reshape(B, 2 * R, FF)
    weights = (
        grad_ada,
        grad_q[:, :, : 3 * D].astype(f32),
        grad_q[:, :, 3 * D :].astype(f32),
        grad_u.reshape(B, 2 * R, FF).astype(f32),
        grad_d.reshape(B, 8 * R, D).astype(f32),
    )
    if lax.axis_size("dp") > GROUP:
        first = lax.axis_index("dp") % GROUP == 0
        weights = lax.psum(tuple(jnp.where(first, w, 0.0) for w in weights), "dp")
    return (output.reshape(I, L, D), grad_tokens.reshape(I, L, D), grad_cond, *weights)


def solution(mesh):
    slots = P(("dp", "fsdp"), None, None)
    weight = P(None, "fsdp", None)
    return jax.shard_map(
        functools.partial(body, mesh.shape["fsdp"]),
        mesh=mesh,
        in_specs=(slots, P(("dp", "fsdp"), None), slots, P(("dp", "fsdp"))) + (weight,) * 5,
        out_specs=(slots, slots, P(("dp", "fsdp"), None)) + (weight,) * 5,
        check_vma=False,
    )
```

time: 714 us -> 169 us (0.24); the launches traced: 703 us -> 169 us
  waiting for transfers between devices: 373 us -> 0 us
  Pallas kernels: 0 us -> 158 us
  matrix products: 141 us -> 0 us
  blocking collectives: 90.4 us -> 0 us
  other arithmetic: 45.5 us -> 6.05 us
  local copies, waits for them, and re-layouts: 37 us -> 4.16 us
  between operations: 15.6 us -> 0.67 us
    reduce_scatter x10 -> x0, waiting for transfers between devices: 205 us -> none  [the longest x2 77.5 us: body(): lax.psum_scatter(g_ada.astype(jnp.bfloat16), 'fsdp', scatter_dimension=0,...]
    pallas_call x0 -> x1, Pallas kernels: none -> 158 us  [body(): pl.pallas_call(functools.partial(kernel, names, F, I, L, D, FF, B), name=...]
    dot_general x42 -> x0, matrix products: 141 us -> none  [the longest x2 13.9 us: block_backward(): jnp.einsum('iqhe,ikhe->ihqk', d_mixed, values, preferred_element_type=jnp...]
    all_gather x4 -> x0, blocking collectives: 90.4 us -> none  [the longest x2 54.4 us: body(): lax.all_gather(w_qkv[index], 'fsdp', axis=0, tiled=True)]
    psum x1 -> x0, waiting for transfers between devices: 89.1 us -> none  [body(): lax.psum((stacked[0], stacked[1], stacked[2], stacked[3], stacked[4]), 'dp')]
    all_gather x6 -> x0, waiting for transfers between devices: 77 us -> none  [the longest x2 51.6 us: body(): lax.all_gather(w_down[index], 'fsdp', axis=0, tiled=True)]
    unnamed x207 -> x16, local copies, waits for them, and re-layouts: 19.3 us -> 4.16 us
    convert_element_type x4 -> x0, local copies, waits for them, and re-layouts: 13.2 us -> none  [the longest x2 8.62 us: block_forward(): jnp.einsum('ild,de->ile', first_in, w_qkv, preferred_element_type=jnp.flo...]
  transfers between devices with their start and end apart: 17 -> 0, of which waited for: 13 -> 0; matrix products, arithmetic and copies ran while one was open for 22% -> 0% of each run, Pallas kernels for 0% -> 0%
where the time goes in v1:
time: 169 us
  Pallas kernels  158 us (93%)
  other arithmetic  6.05 us (4%)
  local copies, waits for them, and re-layouts  4.16 us (2%)
    pallas_call x1, Pallas kernels, body(): pl.pallas_call(functools.partial(kernel, names, F, I, L, D, FF, B), name=...  158 us
    unnamed x16, local copies, waits for them, and re-layouts  4.16 us

profile of v1, /device:TPU:0, one launch (start us, length us, event | category | flops | bytes accessed | tf_op | source)
XLA Modules:
  0.0 168.7 jit_solution(5419922304495068965)
XLA Ops:
  0.6 157.8 %blocks.1 = (bf16[1024,384]{1,0:T(8,128)(2,1)}, f32[1024,384]{1,0:T(8,128)}, f32[4,384]{1,0:T(4,128)}, f32[2,96,2304]{2,1,0:T(8,128)}, bf16[2,2,48,1536]{3,2,1,0...) custom-call(bf16[1024,384]{1,0:T(8,128)(2,1)} %bitcast.16, bf16[4,384]{1,0:T(4,128)(2,1)} %refs_1_.1, ...), custom_call_target="tpu_custom_call" | custom-call | tf_op jit(solution)/shard_map/blocks/pallas_call | solution.py:716
  158.5 0.0 copy-start.4
  158.5 0.0 copy-start.3
  158.5 2.1 %slice_convert_fusion = f32[2,96,1152]{2,1,0:T(8,128)} fusion(bf16[2,96,1536]{2,1,0:T(8,128)(2,1)} %bitcast.21), kind=kLoop, calls=%fused_computation.2 | loop fusion | flops 221184 | bytes 1327104 | tf_op jit(solution)/shard_map/convert_element_type | solution.py:750
  160.6 1.6 slice_convert_fusion.1
  162.2 0.0 copy-done.4
  162.2 0.0 copy-start.2
  162.2 1.2 bitcast_convert_fusion.1
  163.4 0.0 copy-done.3
  163.4 0.0 copy-start.1
  163.4 1.1 bitcast_convert_fusion
  164.6 0.0 copy-done.2
  164.6 0.9 copy.21
  165.5 0.0 copy-done.1
  165.5 0.0 copy-start.5
  165.5 0.0 copy-start
  165.5 1.1 copy.22
  166.6 0.0 copy-done.5
  166.6 0.6 copy.23
  167.2 0.3 copy-done
  167.5 1.2 copy.24
Async XLA Ops:
  158.5 3.7 %copy-start.4 = (bf16[2,2,48,1536]{3,2,1,0:T(8,128)(2,1)S(1)}, bf16[2,2,48,1536]{3,2,1,0:T(8,128)(2,1)}, u32[]{:S(2)}) copy-start(bf16[2,2,48,1536]{3,2,1,0:T(8,128)(2,1)} %get-tuple-element.20) | copy-start | bytes 1769476
  158.5 4.9 %copy-start.3 = (bf16[2,4,2,48,384]{4,3,2,1,0:T(8,128)(2,1)S(1)}, bf16[2,4,2,48,384]{4,3,2,1,0:T(8,128)(2,1)}, u32[]{:S(2)}) copy-start(bf16[2,4,2,48,384]{4,3,2,1,0:T(8,128)(2,1)} %get-tuple-element.21) | copy-start | bytes 1769476
  162.2 2.3 %copy-start.2 = (bf16[1024,384]{1,0:T(8,128)(2,1)S(1)}, bf16[1024,384]{1,0:T(8,128)(2,1)}, u32[]{:S(2)}) copy-start(bf16[1024,384]{1,0:T(8,128)(2,1)} %get-tuple-element.15) | copy-start | bytes 2359300
  163.4 2.0 %copy-start.1 = (f32[1024,384]{1,0:T(8,128)S(1)}, f32[1024,384]{1,0:T(8,128)}, u32[]{:S(2)}) copy-start(f32[1024,384]{1,0:T(8,128)} %get-tuple-element.16) | copy-start | bytes 4718596
  165.5 1.1 copy-start.5
  165.5 2.1 %copy-start = (f32[2,96,2304]{2,1,0:T(8,128)S(1)}, f32[2,96,2304]{2,1,0:T(8,128)}, u32[]{:S(2)}) copy-start(f32[2,96,2304]{2,1,0:T(8,128)} %get-tuple-element.33) | copy-start | bytes 5308420
